TPU v7x, 512 devices: a whole 4x4x16 slice. The times are simulated.
512 devices in a mesh: sp: 64 (over z, x), dp: 8 (over y, core).
Axes of the slice: x: 4, y: 4, z: 16, core: 2. Of those that a mesh axis runs over, the one named last changes fastest.
Arguments:
- hidden_in: bfloat16 [49152, 1024], P(('dp', 'sp')), parts along dimension 0, may hold values from -6 to 6
- queries: bfloat16 [49152, 2048], P(('dp', 'sp')), parts along dimension 0, may hold values from -6 to 6
- keys: bfloat16 [49152, 256], P(('dp', 'sp')), parts along dimension 0, may hold values from -6 to 6
- values: bfloat16 [49152, 256], P(('dp', 'sp')), parts along dimension 0, may hold values from -6 to 6
- q_gain: float32 [128], replicated, may hold values from 0.5 to 1.5
- k_gain: float32 [128], replicated, may hold values from 0.5 to 1.5
- out_weight: bfloat16 [2048, 1024], P(None, 'sp'), may hold values from -0.125 to 0.125
- moe_gain: float32 [1024], replicated, may hold values from 0.5 to 1.5
- expert_ids: int32 [49152, 8], P(('dp', 'sp')), parts along dimension 0, may hold values from 0 to 63, all different within a row; in each aligned block of 96 rows (0 to 95, 96 to 191, ...) at most 15 rows name the same one
- route_weights: float32 [49152, 8], P(('dp', 'sp')), parts along dimension 0, may hold values from 0.05 to 1
- gate_proj: bfloat16 [64, 1024, 384], P('sp'), may hold values from -0.1875 to 0.1875
- up_proj: bfloat16 [64, 1024, 384], P('sp'), may hold values from -0.1875 to 0.1875
- down_proj: bfloat16 [64, 384, 1024], P('sp'), may hold values from -0.3125 to 0.3125
Outputs:
- layer_out: bfloat16 [49152, 1024], P(('dp', 'sp')), parts along dimension 0
There are 8 independent parts, one for each index of `dp`. A program takes and returns all parts, laid end to end along the dimension named above; an argument that names none is the same for every part. Nothing has to cross between parts.
Inputs may be any that keep to these rules, and one draw needn't show every extreme that they name: `expert_ids`: each row names 8 different experts. Among the rows of one index of sp no expert is named more than 15 times; some expert is named exactly 15 times.
All inputs are finite; a program needn't handle non-finite values.
Results may differ from a plain program's by a relative error of at most 0.0075.
Values may be sent and summed in bfloat16 or wider, within the bound.
A program may use at most 128 MiB of HBM per device.

v0:
```python
import math

import jax
import jax.numpy as jnp
from jax import lax
from jax.sharding import PartitionSpec as P

EPS = 1e-06
THETA = 1000000.0


def head_norm(values_in, gain):
    meansq = jnp.mean(values_in * values_in, axis=-1, keepdims=True)
    return values_in * lax.rsqrt(meansq + EPS) * gain


def rotate(values_in, positions):
    half = values_in.shape[-1] // 2
    expo = jnp.arange(half).astype(jnp.float32) * (-2.0 / values_in.shape[-1])
    freq = jnp.power(jnp.float32(THETA), expo)
    angle = positions.astype(jnp.float32)[:, None] * freq[None, :]
    cosv = jnp.cos(angle)[:, None, :]
    sinv = jnp.sin(angle)[:, None, :]
    first = values_in[..., :half]
    second = values_in[..., half:]
    return jnp.concatenate([first * cosv - second * sinv, second * cosv + first * sinv], axis=-1)


def body(
    hidden_in,
    queries,
    keys,
    values,
    q_gain,
    k_gain,
    out_weight,
    moe_gain,
    expert_ids,
    route_weights,
    gate_proj,
    up_proj,
    down_proj,
):
    tok_rows = hidden_in.shape[0]
    width = hidden_in.shape[1]
    head_dim = q_gain.shape[0]
    q_count = queries.shape[1] // head_dim
    kv_count = keys.shape[1] // head_dim
    group = q_count // kv_count
    devices_sp = lax.axis_size("sp")
    positions = lax.axis_index("sp") * tok_rows + jnp.arange(tok_rows, dtype=jnp.int32)
    q_rot = rotate(
        head_norm(queries.astype(jnp.float32).reshape(tok_rows, q_count, head_dim), q_gain),
        positions,
    ).astype(jnp.bfloat16)
    k_rot = rotate(
        head_norm(keys.astype(jnp.float32).reshape(tok_rows, kv_count, head_dim), k_gain), positions
    ).astype(jnp.bfloat16)
    q_grouped = q_rot.reshape(tok_rows, kv_count, group, head_dim)
    k_flat = k_rot.reshape(tok_rows, kv_count * head_dim)
    scale = 1.0 / math.sqrt(head_dim)

    def attend_block(carry, k_piece, v_piece, start):
        numer, denom = carry
        rows = k_piece.shape[0]
        k_piece = k_piece.reshape(rows, kv_count, head_dim)
        v_piece = v_piece.reshape(rows, kv_count, head_dim)
        scores = (
            jnp.einsum("tkgd,skd->kgts", q_grouped, k_piece, preferred_element_type=jnp.float32)
            * scale
        )
        key_pos = start + jnp.arange(rows, dtype=jnp.int32)
        causal = positions[:, None] >= key_pos[None, :]
        expw = jnp.where(causal, jnp.exp(scores), 0.0)
        numer = numer + jnp.einsum(
            "kgts,skd->tkgd", expw.astype(jnp.bfloat16), v_piece, preferred_element_type=jnp.float32
        )
        denom = denom + jnp.sum(expw, axis=-1)
        return (numer, denom)

    start_numer = jnp.zeros((tok_rows, kv_count, group, head_dim), jnp.float32)
    start_denom = jnp.zeros((kv_count, group, tok_rows), jnp.float32)
    k_piece = lax.all_gather(k_flat, "sp", axis=0, tiled=True)
    v_piece = lax.all_gather(values, "sp", axis=0, tiled=True)
    rows = k_piece.shape[0]
    steps = rows // 512

    def one_step(index, inner):
        offset = (index * 512).astype(jnp.int32)
        k_block = lax.dynamic_slice_in_dim(k_piece, offset, 512, 0)
        v_block = lax.dynamic_slice_in_dim(v_piece, offset, 512, 0)
        return attend_block(inner, k_block, v_block, offset)

    numer, denom = lax.fori_loop(0, steps, one_step, (start_numer, start_denom))
    context = (
        (numer / jnp.transpose(denom, (2, 0, 1))[..., None])
        .reshape(tok_rows, q_count * head_dim)
        .astype(jnp.bfloat16)
    )
    attn_out = jnp.dot(
        context,
        lax.all_gather(out_weight, "sp", axis=1, tiled=True),
        preferred_element_type=jnp.float32,
    ).astype(jnp.bfloat16)
    resid = hidden_in.astype(jnp.float32) + attn_out.astype(jnp.float32)
    meansq = jnp.mean(resid * resid, axis=-1, keepdims=True)
    normed = (resid * lax.rsqrt(meansq + EPS) * moe_gain).astype(jnp.bfloat16)
    local_count = gate_proj.shape[0]
    experts_all = devices_sp * local_count
    top = expert_ids.shape[1]
    capacity = max(2, 5 * tok_rows * top // (4 * experts_all))
    flat_ids = expert_ids.reshape(-1)
    onehot = (flat_ids[:, None] == jnp.arange(experts_all, dtype=jnp.int32)[None, :]).astype(
        jnp.int32
    )
    before = jnp.cumsum(onehot, axis=0) - onehot
    slot = jnp.sum(before * onehot, axis=1)
    target = flat_ids * capacity + slot
    placed = jnp.arange(experts_all * capacity, dtype=jnp.int32)[:, None] == target[None, :]
    dispatch = jnp.any(placed.reshape(experts_all * capacity, tok_rows, top), axis=-1).astype(
        jnp.bfloat16
    )
    outgoing = jnp.dot(dispatch, normed, preferred_element_type=jnp.float32).astype(jnp.bfloat16)
    outgoing = outgoing.reshape(devices_sp, local_count, capacity, width)
    block = lax.all_to_all(outgoing, "sp", split_axis=0, concat_axis=0, tiled=True)
    gate = jnp.einsum("nekd,edf->nekf", block, gate_proj, preferred_element_type=jnp.float32)
    upv = jnp.einsum("nekd,edf->nekf", block, up_proj, preferred_element_type=jnp.float32)
    mid = (jax.nn.silu(gate) * upv).astype(jnp.bfloat16)
    result = jnp.einsum(
        "nekf,efd->nekd", mid, down_proj, preferred_element_type=jnp.float32
    ).astype(jnp.bfloat16)
    returned = lax.all_to_all(result, "sp", split_axis=0, concat_axis=0, tiled=True)
    flat_back = returned.reshape(experts_all * capacity, width)
    picked = flat_back[target].astype(jnp.float32).reshape(tok_rows, top, width)
    coef = route_weights / jnp.sum(route_weights, axis=-1, keepdims=True)
    mixed = jnp.sum(picked * coef[:, :, None], axis=1)
    return (resid + mixed).astype(jnp.bfloat16)


def solution(mesh):
    return jax.shard_map(
        body,
        mesh=mesh,
        in_specs=(
            P(("dp", "sp"), None),
            P(("dp", "sp"), None),
            P(("dp", "sp"), None),
            P(("dp", "sp"), None),
            P(),
            P(),
            P(None, "sp"),
            P(),
            P(("dp", "sp"), None),
            P(("dp", "sp"), None),
            P("sp", None, None),
            P("sp", None, None),
            P("sp", None, None),
        ),
        out_specs=P(("dp", "sp"), None),
        check_vma=False,
    )
```

profile of v0, /device:TPU:2, one launch (start us, length us, event | category | flops | bytes accessed | tf_op | source)
XLA Modules:
  0.0 679.2 jit_solution(7008264672583019977)
XLA Ops:
  14.9 1.8 reduce-window.6
  18.5 138.7 %all-gather.6.cloned.1.call-done = bf16[6144,256]{1,0:T(8,128)(2,1)} async-done(((bf16[96,256]{1,0:T(8,128)(2,1)}), bf16[6144,256]{1,0:T(8,128)(2,1)}) %all-gather.6.cloned.1.call-update) | async-done | bytes 3145744 | tf_op jit(solution)/shard_map/all_gather | solution.py:83
  157.1 141.4 %all-gather.4.cloned.1.call-done = bf16[6144,256]{1,0:T(8,128)(2,1)} async-done(((bf16[96,256]{1,0:T(8,128)(2,1)}), bf16[6144,256]{1,0:T(8,128)(2,1)}) %all-gather.4.cloned.1.call-update) | async-done | bytes 3145744 | tf_op jit(solution)/shard_map/all_gather | solution.py:84
  298.5 80.4 %while.16 = (s32[]{:T(128)}, f32[96,2,8,128]{3,0,2,1:T(8,128)S(1)}, f32[2,8,96]{2,1,0:T(8,128)S(1)}, bf16[6144,256]{1,0:T(8,128)(2,1)}, bf16[6144,256]{1,0:T(8,1...) while((s32[]{:T(128)}, f32[96,2,8,128]{3,0,2,1:T(8,128)S(1)}, ...), condition=%wide.region_4.5_spmd.clone, body=%wide.region_2.4_spmd.clone.sunk | while | flops 407816288 | bytes 11056050 | solution.py:94
  299.9 2.5 fusion.69
  302.5 2.7 fusion.70
  306.6 2.5 fusion.69
  309.2 2.6 fusion.70
  313.3 2.5 fusion.69
  315.9 2.6 fusion.70
  318.6 1.1 constant_dynamic-slice_fusion.3
  320.0 2.5 fusion.69
  322.6 2.7 fusion.70
  325.3 1.1 constant_dynamic-slice_fusion.3
  326.7 2.5 fusion.69
  329.3 2.7 fusion.70
  333.4 2.5 fusion.69
  336.0 2.6 fusion.70
  340.1 2.5 fusion.69
  342.7 2.6 fusion.70
  345.4 1.1 constant_dynamic-slice_fusion.3
  346.8 2.5 fusion.69
  349.4 2.6 fusion.70
  352.1 1.1 constant_dynamic-slice_fusion.3
  353.5 2.5 fusion.69
  356.1 2.7 fusion.70
  358.8 1.1 constant_dynamic-slice_fusion.3
  360.2 2.5 fusion.69
  362.8 2.7 fusion.70
  366.9 2.5 fusion.69
  369.5 2.6 fusion.70
  372.2 1.1 constant_dynamic-slice_fusion.3
  373.6 2.5 fusion.69
  376.2 2.6 fusion.70
  379.3 63.5 %all-gather.8.cloned.1.call-done = bf16[2048,1024]{0,1:T(8,128)(2,1)} async-done(((bf16[2048,16]{0,1:T(8,128)(2,1)}), bf16[2048,1024]{0,1:T(8,128)(2,1)}) %all-gather.8.cloned.1.call-update) | async-done | bytes 4194320 | tf_op jit(solution)/shard_map/all_gather | solution.py:102
  442.8 3.7 multiply_reduce_fusion.1
  446.6 2.0 convolution_convert_fusion
  448.6 2.6 reshape.227
  451.2 102.0 %all_to_all.10 = bf16[64,1,15,1024]{3,2,1,0:T(8,128)(2,1)S(1)} all-to-all(bf16[64,1,15,1024]{3,2,1,0:T(8,128)(2,1)S(1)} %bitcast.156), channel_id=1, replica_groups=mesh['sp'=64,'dp'=8] {'sp'}, dimensions={0} | all-to-all | bytes 3932160 | tf_op jit(solution)/shard_map/all_to_all | solution.py:125
  553.3 1.3 copy-done.1
  554.6 2.6 fusion.21
  557.2 4.9 convert_bitcast_fusion
  562.1 2.4 copy.80
  564.5 6.3 all-to-all-start.1
  571.0 92.3 %all-to-all-done.1 = bf16[64,1,15,1024]{3,2,1,0:T(8,128)(2,1)} async-done(((bf16[64,1,15,1024]{3,2,1,0:T(8,128)(2,1)}), bf16[64,1,15,1024]{3,2,1,0:T(8,128)(2,1)}, u32[]{:S(2)}, u32[]{:S(2)}) %all-to-all-start.1) | async-done | bytes 1966112 | tf_op jit(solution)/shard_map/all_to_all | solution.py:132
  663.3 2.6 reshape.233
  665.9 3.6 gather_fusion
  669.5 2.4 fusion.17
  (140 shorter events, 22.5 us)
Async XLA Ops:
  6.5 550.7 %copy-start = (bf16[1,384,1024]{2,1,0:T(8,128)(2,1)S(1)}, bf16[1,384,1024]{2,1,0:T(8,128)(2,1)}, u32[]{:S(2)}) copy-start(bf16[1,384,1024]{2,1,0:T(8,128)(2,1)} %param.27) | copy-start | bytes 2359300
  6.5 150.6 %all-gather.6.cloned.1.call-start = ((), (), s32[]{:S(2)}) async-start(), calls=%async_computation.3 | async-start | bytes 3194880 | tf_op jit(solution)/shard_map/all_gather | solution.py:83
  9.1 4.8 copy-start.5
  9.8 288.7 %all-gather.4.cloned.1.call-start = ((), (), s32[]{:S(2)}) async-start(), calls=%async_computation.2 | async-start | bytes 3194880 | tf_op jit(solution)/shard_map/all_gather | solution.py:84
  10.6 432.3 %all-gather.8.cloned.1.call-start = ((), (), s32[]{:S(2)}) async-start(), calls=%async_computation.4 | async-start | bytes 4259840 | tf_op jit(solution)/shard_map/all_gather | solution.py:102
  378.9 64.0 %copy-start.2 = (bf16[96,1024]{1,0:T(8,128)(2,1)S(1)}, bf16[96,1024]{1,0:T(8,128)(2,1)}, u32[]{:S(2)}) copy-start(bf16[96,1024]{1,0:T(8,128)(2,1)} %param.15) | copy-start | bytes 589828
  442.8 3.8 copy-start.4
  451.2 103.4 %copy-start.6 = (bf16[1,1024,384]{2,1,0:T(8,128)(2,1)S(1)}, bf16[1,1024,384]{2,1,0:T(8,128)(2,1)}, u32[]{:S(2)}) copy-start(bf16[1,1024,384]{2,1,0:T(8,128)(2,1)} %param.25) | copy-start | bytes 2359300
  553.3 1.4 copy-start.1
  564.5 6.4 copy-start.3
  564.5 98.8 %all-to-all-start.1 = ((bf16[64,1,15,1024]{3,2,1,0:T(8,128)(2,1)}), bf16[64,1,15,1024]{3,2,1,0:T(8,128)(2,1)}, u32[]{:S(2)}, u32[]{:S(2)}) async-start(bf16[64,1,15,1024]{3,2,1,0:T(8,128)(2,1)} %copy.80), calls=%async_computation.1 | async-start | bytes 4194304 | tf_op jit(solution)/shard_map/all_to_all | solution.py:132
Sparse Core Ops, SparseCore 0:
  10.3 146.7 all-gather.5
  160.1 138.3 all-gather.3
  301.5 141.3 all-gather.7
where the time goes:
time: 680 us; the launch traced here: 679 us
  waiting for transfers between devices  437 us (64%)
  blocking collectives  102 us (15%)
  matrix products  75.1 us (11%)
  local copies, waits for them, and re-layouts  32.4 us (5%)
  between operations  13.4 us (2%)
  other arithmetic  11.7 us (2%)
    all_gather x1, waiting for transfers between devices, body(): v_piece = lax.all_gather(values, 'sp', axis=0, tiled=True)  141 us
    all_gather x1, waiting for transfers between devices, body(): k_piece = lax.all_gather(k_flat, 'sp', axis=0, tiled=True)  139 us
    all_to_all x1, blocking collectives, body(): lax.all_to_all(outgoing, 'sp', split_axis=0, concat_axis=0, tiled=True)  102 us
    all_to_all x1, waiting for transfers between devices, body(): lax.all_to_all(result, 'sp', split_axis=0, concat_axis=0, tiled=True)  92.3 us
    all_gather x1, waiting for transfers between devices, body(): lax.all_gather(out_weight, 'sp', axis=1, tiled=True)  63.5 us
    dot_general x12, matrix products, attend_block(): jnp.einsum('kgts,skd->tkgd', expw.astype(jnp.bfloat16), v_piece, preferre...  31.8 us
    dot_general x12, matrix products, attend_block(): jnp.einsum('tkgd,skd->kgts', q_grouped, k_piece, preferred_element_type=j...  30.1 us
    dynamic_slice x24, local copies, waits for them, and re-layouts, one_step(): k_block = lax.dynamic_slice_in_dim(k_piece, offset, 512, 0)  14.5 us
  transfers between devices with their start and end apart: 4, of which 4 were waited for; matrix products, arithmetic and copies ran while one was open for 13% of the time, Pallas kernels for 0%

commit v1 on v0

v1 whole, which is shorter than its diff:
```python
import functools
import math

import jax
import jax.numpy as jnp
from jax import lax
from jax.experimental import pallas as pl
from jax.experimental.pallas import tpu as pltpu
from jax.sharding import PartitionSpec as P

EPS = 1e-06
THETA = 1000000.0
MESH = pl.DeviceIdType.MESH
F32 = jnp.float32
BF16 = jnp.bfloat16

TOK = 96
ZN = 16
SLOT = 16
PIECES = ((64, 16), (64, 16), (32, 12))
NPIECE = 44
FIRST, PER_STEP, PER_HOP = 6, 2, 3
NT = (((1,), (1,)), ((), ()))


def dot(a, b):
    return jnp.dot(a, b, preferred_element_type=F32)


def dot_nt(a, b):
    return lax.dot_general(a, b, NT, preferred_element_type=F32)


def copy_to(src, dst, send, recv, sp, dp):
    return pltpu.make_async_remote_copy(
        src_ref=src, dst_ref=dst, send_sem=send, recv_sem=recv,
        device_id={"sp": sp, "dp": dp}, device_id_type=MESH,
    )


def place():
    sp = lax.axis_index("sp")
    g = lax.axis_index("dp")
    z = sp // 4
    x = sp % 4
    return z, x, g, g // 2, g % 2


def signal(sem, sp, dp):
    pl.semaphore_signal(sem, inc=1, device_id={"sp": sp, "dp": dp}, device_id_type=MESH)


def route_kernel(ids_ref, idst_ref, rw_ref, d_ref, c_ref):
    slots = 64 * SLOT
    top = ids_ref.shape[1]

    def order(e):
        return (e & 31) * 2 + (e >> 5)

    ids = order(ids_ref[...])
    idst = order(idst_ref[...])
    rw = rw_ref[...]
    coef = rw / jnp.sum(rw, axis=-1, keepdims=True)
    mt = jnp.zeros((64, TOK), F32)
    m = jnp.zeros((TOK, 64), F32)
    cm = jnp.zeros((TOK, 64), F32)
    e0 = lax.broadcasted_iota(jnp.int32, (64, TOK), 0)
    e1 = lax.broadcasted_iota(jnp.int32, (TOK, 64), 1)
    for k in range(top):
        mt = mt + jnp.where(idst[k : k + 1, :] == e0, 1.0, 0.0)
        hit = ids[:, k : k + 1] == e1
        m = m + jnp.where(hit, 1.0, 0.0)
        cm = cm + jnp.where(hit, coef[:, k : k + 1], 0.0)
    r = lax.broadcasted_iota(jnp.int32, (TOK, TOK), 0)
    q = lax.broadcasted_iota(jnp.int32, (TOK, TOK), 1)
    upper = jnp.where(r < q, 1.0, 0.0).astype(BF16)
    lower = jnp.where(q < r, 1.0, 0.0).astype(BF16)
    mtb = mt.astype(BF16)
    mb = m.astype(BF16)
    post = dot(mtb, upper).astype(BF16)
    pos = dot(lower, mb).astype(BF16)
    s0 = lax.broadcasted_iota(jnp.int32, (slots, 64), 0)
    x1 = lax.broadcasted_iota(jnp.int32, (slots, 64), 1)
    rep = jnp.where((s0 >> 4) == x1, 1.0, 0.0).astype(BF16)
    x0 = lax.broadcasted_iota(jnp.int32, (64, slots), 0)
    s1 = lax.broadcasted_iota(jnp.int32, (64, slots), 1)
    rept = jnp.where((s1 >> 4) == x0, 1.0, 0.0).astype(BF16)
    lane = (lax.broadcasted_iota(jnp.int32, (slots, TOK), 0) & 15).astype(F32)
    d_ref[...] = jnp.where(dot(rep, mtb) > 0.5, jnp.where(dot(rep, post) == lane, 1.0, 0.0), 0.0).astype(BF16)
    lanet = (lax.broadcasted_iota(jnp.int32, (TOK, slots), 1) & 15).astype(F32)
    keep = jnp.where(dot(mb, rept) > 0.5, jnp.where(dot(pos, rept) == lanet, 1.0, 0.0), 0.0)
    hi = cm.astype(BF16)
    lo = (cm - hi.astype(F32)).astype(BF16)
    c_ref[0:TOK, :] = (dot(hi, rept) * keep).astype(BF16)
    c_ref[TOK : 2 * TOK, :] = (dot(lo, rept) * keep).astype(BF16)


def layer_kernel(
    q_ref, k_ref, v_ref, qg_ref, kg_ref, cos_ref, sin_ref, wt_ref,
    hid_ref, gain_ref, d_ref, c_ref, gate_ref, up_ref, down_ref,
    out_ref,
    qsend, kvsend, qbuf, qall, kvbuf, acc, den, ctx, wz, wfull, pstage, pbuf,
    resid, outb, inb, yb, retb, wg, wu, wd,
    q_s, q_r, kv_s, kv_r, up_s, up_r, dn_s, dn_r, sib_s, sib_r, wz_s, wz_r, wf_s, wf_r, p_s, p_r,
    own_sem, wup_s, wup_r, wdn_s, wdn_r, loc, a_s, a_r, b_s, b_r,
):
    z, x, g, y, c = place()
    sp = z * 4 + x
    q_idx = g * 4 + x
    up_sp = ((z + 1) % ZN) * 4 + x
    dn_sp = ((z + ZN - 1) % ZN) * 4 + x
    sib = y * 2 + (1 - c)
    is_self = c == x // 2
    own_k = z // 8
    source = z % 8 == g
    inner = jnp.logical_not(source)
    p_ring = (z - g + ZN) % ZN

    barrier = pltpu.get_barrier_semaphore()

    def loop(lo, hi, fn):
        def one(i, carry):
            fn(i)
            return carry

        lax.fori_loop(lo, hi, one, 0)

    loop(1, ZN, lambda o: signal(barrier, ((z + o) % ZN) * 4 + x, g))

    def slice_peer(o):
        t = (q_idx + o) % 32
        return t, z * 4 + t % 4, t // 4

    def greet(o):
        t, psp, pdp = slice_peer(o)
        signal(barrier, psp, pdp)

    loop(1, 32, greet)

    stores = (wg, wu, wd)
    own = [
        pltpu.make_async_copy(src, dst.at[own_k], own_sem.at[i])
        for i, (src, dst) in enumerate(zip((gate_ref, up_ref, down_ref), stores))
    ]

    @pl.when(source)
    def _():
        for copy in own:
            copy.start()

    cosv = cos_ref[...]
    sinv = sin_ref[...]

    def turned(val, gain):
        val = val.astype(F32)
        ms = jnp.mean(val * val, axis=-1, keepdims=True)
        n = val * lax.rsqrt(ms + EPS) * gain
        return (n * cosv + pltpu.roll(n, 64, 1) * sinv).astype(BF16)

    for h in range(2):
        kvsend[h, :, 0:128] = turned(k_ref[:, h * 128 : (h + 1) * 128], kg_ref[...])
        kvsend[h, :, 128:256] = v_ref[:, h * 128 : (h + 1) * 128]
    for h in range(2):
        for n in range(8):
            at = (h * 8 + n) * 128
            qsend[h, :, n * 128 : (n + 1) * 128] = turned(q_ref[:, at : at + 128], qg_ref[...])

    pl.semaphore_wait(barrier, 46)

    rows = pl.ds(pl.multiple_of((x % 2) * TOK, TOK), TOK)
    dest_dp = y * 2 + x // 2
    for h in range(2):
        dest_sp = z * 4 + 2 * c + h
        here = jnp.logical_and(is_self, x % 2 == h)
        kv_dst = kvbuf.at[z, x // 2, rows, :]
        q_dst = qbuf.at[x % 2]

        @pl.when(here)
        def _():
            pltpu.make_async_copy(kvsend.at[h], kv_dst, kv_r.at[x % 2]).start()
            pltpu.make_async_copy(qsend.at[h], q_dst, q_r.at[x % 2]).start()

        @pl.when(jnp.logical_not(here))
        def _():
            copy_to(kvsend.at[h], kv_dst, kv_s.at[h], kv_r.at[x % 2], dest_sp, dest_dp).start()
            copy_to(qsend.at[h], q_dst, q_s.at[h], q_r.at[x % 2], dest_sp, dest_dp).start()

    def wz_copy(o):
        return copy_to(wt_ref, wz.at[own_k], wz_s.at[o], wz_r.at[own_k], ((z + o) % ZN) * 4 + x, g)

    @pl.when(source)
    def _():
        wz[own_k] = wt_ref[...]
        loop(1, ZN, lambda o: wz_copy(o).start())

    k_up = p_ring // 8
    k_dn = jnp.where(source, k_up, 1 - k_up)
    k_up_in = ((p_ring + ZN - 1) % ZN) // 8
    far_up = p_ring % 8
    far_dn = (ZN - p_ring) % 8
    down = far_dn != 7

    def piece(j, fn):
        at = 0
        for store, (n_rows, count) in zip(stores, PIECES):
            first = at

            @pl.when(jnp.logical_and(j >= first, j < first + count))
            def _():
                start = pl.multiple_of((j - first) * n_rows, n_rows)
                fn(lambda k: store.at[k, pl.ds(start, n_rows), :])

            at += count

    def wup(ref, j):
        return copy_to(ref, ref, wup_s.at[j], wup_r.at[j], up_sp, g)

    def wdn(ref, j):
        return copy_to(ref, ref, wdn_s.at[j], wdn_r.at[j], dn_sp, g)

    def one_up(j):
        def act(ref):
            @pl.when(inner)
            def _():
                wup(ref(k_up_in), j).wait_recv()

            wup(ref(k_up), j).start()

        piece(j, act)

    def one_dn(j):
        def act(ref):
            @pl.when(inner)
            def _():
                wdn(ref(k_dn), j).wait_recv()

            @pl.when(down)
            def _():
                wdn(ref(k_dn), j).start()

        piece(j, act)

    def reach(t, far):
        return jnp.clip(FIRST + PER_STEP * t - PER_HOP * far, 0, NPIECE)

    def ring(t):
        for far, act in ((far_up, one_up), (far_dn, one_dn)):
            lo = jnp.where(jnp.logical_and(t == 0, inner), 0, reach(t, far))
            loop(lo, reach(t + 1, far), act)

    @pl.when(source)
    def _():
        for copy in own:
            copy.wait()
        loop(0, FIRST, one_up)
        loop(0, FIRST, one_dn)


    for t in range(2):
        kdst = kvbuf.at[z, c, pl.ds(t * TOK, TOK), :]
        pltpu.make_async_copy(kdst, kdst, kv_r.at[t]).wait()

    def up_copy(s, slice_idx):
        ref = kvbuf.at[slice_idx, c]
        return copy_to(ref, ref, up_s.at[s], up_r.at[s], up_sp, g)

    def dn_copy(s, slice_idx):
        ref = kvbuf.at[slice_idx, c]
        return copy_to(ref, ref, dn_s.at[s], dn_r.at[s], dn_sp, g)

    def sib_copy(i, slice_idx, half):
        ref = kvbuf.at[slice_idx, half]
        return copy_to(ref, ref, sib_s.at[i], sib_r.at[i], sp, sib)

    up_copy(1, z).start()
    dn_copy(1, z).start()
    sib_copy(0, z, c).start()

    for t in range(2):
        pltpu.make_async_copy(qbuf.at[t], qbuf.at[t], q_r.at[t]).wait()
    for n in range(8):
        for t in range(2):
            qall[n * 192 + t * TOK : n * 192 + (t + 1) * TOK, :] = qbuf[t, :, n * 128 : (n + 1) * 128]

    factor = math.log2(math.e) / math.sqrt(128)

    def attend(slice_idx, diagonal):
        kv = kvbuf[slice_idx]
        kk = kv[:, :, 0:128].reshape(384, 128)
        vv = kv[:, :, 128:256].reshape(384, 128)
        for n in range(4):
            at = slice(n * 384, (n + 1) * 384)
            s = dot_nt(qall[at, :], kk)
            p = jnp.exp2(s * factor)
            if diagonal:
                r = lax.broadcasted_iota(jnp.int32, (384, 384), 0)
                r = jnp.where(r >= 192, r - 192, r) + c * 192
                col = lax.broadcasted_iota(jnp.int32, (384, 384), 1)
                p = jnp.where(col <= r, p, 0.0)
            part = p[:, 0:128] + p[:, 128:256] + p[:, 256:384]
            pv = dot(p.astype(BF16), vv)
            if diagonal:
                den[at, :] = part
                acc[at, :] = pv
            else:
                den[at, :] = den[at, :] + part
                acc[at, :] = acc[at, :] + pv

    sib_copy(0, z, 1 - c).wait_recv()
    attend(z, True)

    def step(s):
        below = (z - s + ZN) % ZN
        above = (z + s) % ZN
        up_copy(s, below).wait_recv()

        @pl.when(s < 8)
        def _():
            up_copy(s + 1, below).start()

        sib_copy(2 * s, below, c).start()

        @pl.when(s < 8)
        def _():
            dn_copy(s, above).wait_recv()

            @pl.when(s < 7)
            def _():
                dn_copy(s + 1, above).start()

            sib_copy(2 * s + 1, above, c).start()

        ring(s - 1)
        sib_copy(2 * s, below, 1 - c).wait_recv()

        @pl.when(z >= s)
        def _():
            attend(below, False)

        @pl.when(s < 8)
        def _():
            sib_copy(2 * s + 1, above, 1 - c).wait_recv()

            @pl.when(z + s >= ZN)
            def _():
                attend(above, False)

    loop(1, 5, step)

    for k in range(2):

        @pl.when(jnp.logical_not(jnp.logical_and(source, own_k == k)))
        def _():
            pltpu.make_async_copy(wz.at[k], wz.at[k], wz_r.at[k]).wait()

    def wf_copy(o):
        t, psp, pdp = slice_peer(o)
        cols = pl.ds(pl.multiple_of((t % 2) * 1024, 1024), 1024)
        return copy_to(wz.at[:, :, cols], wfull.at[:, q_idx], wf_s.at[o], wf_r.at[o], psp, pdp)

    loop(1, 32, lambda o: wf_copy(o).start())
    mine = pl.ds(pl.multiple_of((x % 2) * 1024, 1024), 1024)
    local = pltpu.make_async_copy(wz.at[:, :, mine], wfull.at[:, q_idx], loc.at[0])
    local.start()

    loop(5, 9, step)

    for n in range(8):
        at = slice(n * 192, (n + 1) * 192)
        total = jnp.sum(den[at, :], axis=-1, keepdims=True)
        ctx[:, n * 128 : (n + 1) * 128] = (acc[at, :] / total).astype(BF16)
    local.wait()
    loop(1, 32, lambda o: wf_copy(o).wait_recv())
    for b in range(4):
        w = wfull[b // 2, (b % 2) * 16 : (b % 2 + 1) * 16].reshape(256, 1024)
        part = dot_nt(ctx[...], w).astype(BF16)
        for t in range(2):
            pstage[t, :, b * 256 : (b + 1) * 256] = part[t * TOK : (t + 1) * TOK, :]
    for t in range(2):
        here = jnp.logical_and(is_self, x % 2 == t)
        dst = pbuf.at[x % 2]

        @pl.when(here)
        def _():
            pltpu.make_async_copy(pstage.at[t], dst, p_r.at[x % 2]).start()

        @pl.when(jnp.logical_not(here))
        def _():
            copy_to(pstage.at[t], dst, p_s.at[t], p_r.at[x % 2], z * 4 + 2 * c + t, dest_dp).start()

    ring(8)
    ring(9)
    for h in range(2):
        pltpu.make_async_copy(pbuf.at[h], pbuf.at[h], p_r.at[h]).wait()

    attn = (pbuf[0].astype(F32) + pbuf[1].astype(F32)).astype(BF16).astype(F32)
    res = hid_ref[...].astype(F32) + attn
    resid[...] = res
    ms = jnp.mean(res * res, axis=-1, keepdims=True)
    normed = (res * lax.rsqrt(ms + EPS) * gain_ref[...]).astype(BF16)

    def there(o):
        t, psp, pdp = slice_peer(o)
        return copy_to(outb.at[t], inb.at[:, q_idx], a_s.at[o], a_r.at[o], psp, pdp)

    def back(o):
        t, psp, pdp = slice_peer(o)
        return copy_to(yb.at[:, t], retb.at[q_idx], b_s.at[o], b_r.at[o], psp, pdp)

    for b in range(4):
        part = dot(d_ref[b * 256 : (b + 1) * 256, :], normed).astype(BF16)
        outb[b * 8 : (b + 1) * 8] = part.reshape(8, 2, SLOT, 1024)
    loop(1, 32, lambda o: there(o).start())
    keep = pltpu.make_async_copy(outb.at[q_idx], inb.at[:, q_idx], loc.at[1])
    keep.start()

    def rest(i):
        for far, act in ((far_up, one_up), (far_dn, one_dn)):
            j = i - PER_HOP * far

            @pl.when(jnp.logical_and(j >= 0, j < NPIECE))
            def _():
                act(j)

    loop(FIRST + PER_STEP * 10, NPIECE + PER_HOP * 7, rest)

    @pl.when(source)
    def _():
        loop(0, NPIECE, lambda j: piece(j, lambda ref: wup(ref(k_up_in), j).wait_recv()))

    keep.wait()
    loop(1, 32, lambda o: there(o).wait_recv())
    for k in range(2):
        tokens = inb[k].reshape(512, 1024)
        gate = dot(tokens, wg[k])
        upv = dot(tokens, wu[k])
        mid = (gate / (1.0 + jnp.exp(-gate)) * upv).astype(BF16)
        yb[k] = dot(mid, wd[k]).astype(BF16).reshape(32, SLOT, 1024)
    loop(1, 32, lambda o: back(o).start())
    keep2 = pltpu.make_async_copy(yb.at[:, q_idx], retb.at[q_idx], loc.at[2])
    keep2.start()

    @pl.when(source)
    def _():
        loop(1, ZN, lambda o: wz_copy(o).wait_send())

    loop(0, NPIECE, lambda j: piece(j, lambda ref: wup(ref(k_up), j).wait_send()))

    @pl.when(down)
    def _():
        loop(0, NPIECE, lambda j: piece(j, lambda ref: wdn(ref(k_dn), j).wait_send()))

    loop(1, 32, lambda o: wf_copy(o).wait_send())
    loop(1, 9, lambda s: up_copy(s, z).wait_send())
    loop(1, 8, lambda s: dn_copy(s, z).wait_send())
    sib_copy(0, z, c).wait_send()
    loop(2, 17, lambda i: sib_copy(i, z, c).wait_send())
    for h in range(2):
        here = jnp.logical_and(is_self, x % 2 == h)

        @pl.when(jnp.logical_not(here))
        def _():
            dst = kvbuf.at[z, x // 2, rows, :]
            dest_sp = z * 4 + 2 * c + h
            copy_to(kvsend.at[h], dst, kv_s.at[h], kv_r.at[x % 2], dest_sp, dest_dp).wait_send()
            copy_to(qsend.at[h], qbuf.at[x % 2], q_s.at[h], q_r.at[x % 2], dest_sp, dest_dp).wait_send()
            copy_to(pstage.at[h], pbuf.at[x % 2], p_s.at[h], p_r.at[x % 2], dest_sp, dest_dp).wait_send()

    loop(1, 32, lambda o: there(o).wait_send())
    keep2.wait()
    loop(1, 32, lambda o: back(o).wait_recv())
    mixed = dot(c_ref[...], retb[...].reshape(1024, 1024))
    out_ref[...] = (resid[...] + (mixed[0:TOK, :] + mixed[TOK : 2 * TOK, :])).astype(BF16)
    loop(1, 32, lambda o: back(o).wait_send())


def body(
    hidden_in, queries, keys, values, q_gain, k_gain, out_weight, moe_gain,
    expert_ids, route_weights, gate_proj, up_proj, down_proj,
):
    sp = lax.axis_index("sp")
    positions = sp * TOK + jnp.arange(TOK, dtype=jnp.int32)
    expo = jnp.arange(64).astype(F32) * (-2.0 / 128)
    freq = jnp.power(jnp.float32(THETA), expo)
    angle = positions.astype(F32)[:, None] * freq[None, :]
    cosv = jnp.cos(angle)
    sinv = jnp.sin(angle)
    cos2 = jnp.concatenate([cosv, cosv], axis=-1)
    sin2 = jnp.concatenate([-sinv, sinv], axis=-1)
    vm = pl.BlockSpec(memory_space=pltpu.VMEM)
    hbm = pl.BlockSpec(memory_space=pl.ANY)
    dma = pltpu.SemaphoreType.DMA

    disp, comb = pl.pallas_call(
        route_kernel,
        out_shape=(jax.ShapeDtypeStruct((1024, TOK), BF16), jax.ShapeDtypeStruct((2 * TOK, 1024), BF16)),
        in_specs=[vm] * 3,
        out_specs=(vm, vm),
        name="route",
    )(expert_ids, expert_ids.T, route_weights)

    return pl.pallas_call(
        layer_kernel,
        out_shape=jax.ShapeDtypeStruct((TOK, 1024), BF16),
        in_specs=[vm] * 12 + [hbm] * 3,
        out_specs=vm,
        scratch_shapes=[
            pltpu.VMEM((2, TOK, 1024), BF16),
            pltpu.VMEM((2, TOK, 256), BF16),
            pltpu.VMEM((2, TOK, 1024), BF16),
            pltpu.VMEM((1536, 128), BF16),
            pltpu.VMEM((ZN, 2, 192, 256), BF16),
            pltpu.VMEM((1536, 128), F32),
            pltpu.VMEM((1536, 128), F32),
            pltpu.VMEM((192, 1024), BF16),
            pltpu.VMEM((2, 16, 2048), BF16),
            pltpu.VMEM((2, 32, 16, 1024), BF16),
            pltpu.VMEM((2, TOK, 1024), BF16),
            pltpu.VMEM((2, TOK, 1024), BF16),
            pltpu.VMEM((TOK, 1024), F32),
            pltpu.VMEM((32, 2, SLOT, 1024), BF16),
            pltpu.VMEM((2, 32, SLOT, 1024), BF16),
            pltpu.VMEM((2, 32, SLOT, 1024), BF16),
            pltpu.VMEM((32, 2, SLOT, 1024), BF16),
            pltpu.VMEM((2, 1024, 384), BF16),
            pltpu.VMEM((2, 1024, 384), BF16),
            pltpu.VMEM((2, 384, 1024), BF16),
            dma((2,)), dma((2,)), dma((2,)), dma((2,)),
            dma((9,)), dma((9,)), dma((9,)), dma((9,)),
            dma((17,)), dma((17,)),
            dma((16,)), dma((2,)), dma((32,)), dma((32,)),
            dma((2,)), dma((2,)), dma((3,)),
            dma((NPIECE,)), dma((NPIECE,)), dma((NPIECE,)), dma((NPIECE,)),
            dma((3,)),
            dma((32,)), dma((32,)), dma((32,)), dma((32,)),
        ],
        compiler_params=pltpu.CompilerParams(
            collective_id=0, has_side_effects=True, vmem_limit_bytes=48 * 1024 * 1024
        ),
        name="layer",
    )(
        queries, keys, values, q_gain.reshape(1, 128), k_gain.reshape(1, 128), cos2, sin2, out_weight.T,
        hidden_in, moe_gain.reshape(1, 1024), disp, comb, gate_proj[0], up_proj[0], down_proj[0],
    )


def solution(mesh):
    tok = P(("dp", "sp"), None)
    return jax.shard_map(
        body,
        mesh=mesh,
        in_specs=(
            tok, tok, tok, tok, P(), P(), P(None, "sp"), P(), tok, tok,
            P("sp", None, None), P("sp", None, None), P("sp", None, None),
        ),
        out_specs=tok,
        check_vma=False,
    )
```

time: 680 us -> 195 us (0.29)
  the two profiles are of different devices: /device:TPU:2 before, /device:TPU:21 now
where the time goes in v1:
time: 195 us; the launch traced here: 194 us
  Pallas kernels  183 us (94%)
  local copies, waits for them, and re-layouts  11.2 us (6%)
    pallas_call x1, Pallas kernels, body(): pl.pallas_call(layer_kernel, out_shape=jax.ShapeDtypeStruct((TOK, 1024),...  180 us
    unnamed x29, local copies, waits for them, and re-layouts  11.2 us

profile of v1, /device:TPU:21, one launch (start us, length us, event | category | flops | bytes accessed | tf_op | source)
XLA Modules:
  0.0 194.2 jit_solution(17190882793835078053)
XLA Ops:
  0.0 0.0 copy-start.3
  0.0 1.4 copy.15.rw_ref
  1.5 1.4 copy.14.ids_ref
  2.9 0.2 fusion
  3.1 0.0 copy-start.6
  3.1 0.1 pad_maximum_fusion
  3.2 0.0 copy-start.8
  3.2 0.0 copy-start.10
  3.3 2.4 %route.1 = (bf16[1024,96]{1,0:T(8,128)(2,1)}, bf16[192,1024]{1,0:T(8,128)(2,1)}) custom-call(s32[96,8]{1,0:T(8,128)} %copy.14.ids_ref, s32[8,96]{1,0:T(8,128)} %bitcast.15, f32[96,8]{1,0:T(8,128)} %copy.15.rw_ref), custom_call_target="tpu_custom_call" | custom-call | tf_op jit(solution)/shard_map/route/pallas_call | solution.py:494
  5.6 0.0 copy-start.11
  5.6 0.0 copy-start.12
  5.7 0.0 copy-done.3
  5.7 0.0 copy-done.6
  5.7 0.0 copy-done.8
  5.7 0.0 copy-done.10
  5.7 0.6 copy-done.11
  6.3 0.0 copy-done.12
  6.3 0.0 copy-start
  6.3 1.1 copy-done
  7.5 0.0 copy-start.1
  7.5 1.1 copy-done.1
  8.6 0.0 copy-start.2
  8.6 1.1 copy-done.2
  9.7 0.0 copy-start.4
  9.7 1.0 copy-done.4
  10.7 0.0 copy-start.5
  10.7 0.9 copy-done.5
  11.7 0.0 copy-start.7
  11.7 0.8 copy-done.7
  12.5 0.0 copy-start.9
  12.5 0.8 copy-done.9
  13.3 180.2 %layer.1 = bf16[96,1024]{1,0:T(8,128)(2,1)S(1)} custom-call(bf16[96,2048]{1,0:T(8,128)(2,1)S(1)} %copy-done.3, bf16[96,256]{1,0:T(8,128)(2,1)S(1)} %copy-done.8, bf16[96,256]{1,0:T(8,128)(2,1)S(1)} %copy-done.9, f32[1,128]{1,0:T(1,128)S(1)} %bitcast.13, f32[1,128]{1,0:T(1,128)S(1)} %bitcast.14, f32[96,128]{1,0:T(8,128)S(1)} %get-tuple-element.12.cos_ref, ...), custom_call_target="tpu_custom_call" | custom-call | tf_op jit(solution)/shard_map/layer/pallas_call | solution.py:502
  193.5 0.7 copy.17
  (2 shorter events, 0.0 us)
Async XLA Ops:
  0.0 5.7 %copy-start.3 = (bf16[96,2048]{1,0:T(8,128)(2,1)S(1)}, bf16[96,2048]{1,0:T(8,128)(2,1)}, u32[]{:S(2)}) copy-start(bf16[96,2048]{1,0:T(8,128)(2,1)} %q_ref.1) | copy-start | bytes 1179652
  3.1 2.5 %copy-start.6 = (bf16[96,1024]{1,0:T(8,128)(2,1)S(1)}, bf16[96,1024]{1,0:T(8,128)(2,1)}, u32[]{:S(2)}) copy-start(bf16[96,1024]{1,0:T(8,128)(2,1)} %hid_ref.1) | copy-start | bytes 589828
  3.2 2.4 %copy-start.8 = (bf16[96,256]{1,0:T(8,128)(2,1)S(1)}, bf16[96,256]{1,0:T(8,128)(2,1)}, u32[]{:S(2)}) copy-start(bf16[96,256]{1,0:T(8,128)(2,1)} %k_ref.1) | copy-start | bytes 147460
  3.2 2.4 %copy-start.10 = (f32[1024]{0:T(1024)S(1)}, f32[1024]{0:T(1024)}, u32[]{:S(2)}) copy-start(f32[1024]{0:T(1024)} %param.20) | copy-start | bytes 12292
  5.6 0.7 copy-start.11
  5.6 0.7 copy-start.12
  6.3 1.1 copy-start
  7.5 1.1 copy-start.1
  8.6 1.1 copy-start.2
  9.7 1.0 copy-start.4
  10.7 0.9 copy-start.5
  11.7 0.8 copy-start.7
  12.5 0.8 copy-start.9

commit v2 on v1

--- a/solution.py
+++ b/solution.py
@@ -50,55 +50,42 @@
     pl.semaphore_signal(sem, inc=1, device_id={"sp": sp, "dp": dp}, device_id_type=MESH)
 
 
-def route_kernel(ids_ref, idst_ref, rw_ref, d_ref, c_ref):
+def route(idst, rwt, d_ref, c_ref):
     slots = 64 * SLOT
-    top = ids_ref.shape[1]
-
-    def order(e):
-        return (e & 31) * 2 + (e >> 5)
-
-    ids = order(ids_ref[...])
-    idst = order(idst_ref[...])
-    rw = rw_ref[...]
-    coef = rw / jnp.sum(rw, axis=-1, keepdims=True)
-    mt = jnp.zeros((64, TOK), F32)
-    m = jnp.zeros((TOK, 64), F32)
-    cm = jnp.zeros((TOK, 64), F32)
-    e0 = lax.broadcasted_iota(jnp.int32, (64, TOK), 0)
-    e1 = lax.broadcasted_iota(jnp.int32, (TOK, 64), 1)
-    for k in range(top):
-        mt = mt + jnp.where(idst[k : k + 1, :] == e0, 1.0, 0.0)
-        hit = ids[:, k : k + 1] == e1
-        m = m + jnp.where(hit, 1.0, 0.0)
-        cm = cm + jnp.where(hit, coef[:, k : k + 1], 0.0)
+    order = (idst & 31) * 2 + (idst >> 5)
+    coef = rwt / jnp.sum(rwt, axis=0, keepdims=True)
+    hits = jnp.zeros((64, TOK), F32)
+    weights = jnp.zeros((64, TOK), F32)
+    expert = lax.broadcasted_iota(jnp.int32, (64, TOK), 0)
+    for k in range(idst.shape[0]):
+        hit = order[k : k + 1, :] == expert
+        hits = hits + jnp.where(hit, 1.0, 0.0)
+        weights = weights + jnp.where(hit, coef[k : k + 1, :], 0.0)
     r = lax.broadcasted_iota(jnp.int32, (TOK, TOK), 0)
     q = lax.broadcasted_iota(jnp.int32, (TOK, TOK), 1)
-    upper = jnp.where(r < q, 1.0, 0.0).astype(BF16)
-    lower = jnp.where(q < r, 1.0, 0.0).astype(BF16)
-    mtb = mt.astype(BF16)
-    mb = m.astype(BF16)
-    post = dot(mtb, upper).astype(BF16)
-    pos = dot(lower, mb).astype(BF16)
-    s0 = lax.broadcasted_iota(jnp.int32, (slots, 64), 0)
-    x1 = lax.broadcasted_iota(jnp.int32, (slots, 64), 1)
-    rep = jnp.where((s0 >> 4) == x1, 1.0, 0.0).astype(BF16)
-    x0 = lax.broadcasted_iota(jnp.int32, (64, slots), 0)
-    s1 = lax.broadcasted_iota(jnp.int32, (64, slots), 1)
-    rept = jnp.where((s1 >> 4) == x0, 1.0, 0.0).astype(BF16)
-    lane = (lax.broadcasted_iota(jnp.int32, (slots, TOK), 0) & 15).astype(F32)
-    d_ref[...] = jnp.where(dot(rep, mtb) > 0.5, jnp.where(dot(rep, post) == lane, 1.0, 0.0), 0.0).astype(BF16)
-    lanet = (lax.broadcasted_iota(jnp.int32, (TOK, slots), 1) & 15).astype(F32)
-    keep = jnp.where(dot(mb, rept) > 0.5, jnp.where(dot(pos, rept) == lanet, 1.0, 0.0), 0.0)
-    hi = cm.astype(BF16)
-    lo = (cm - hi.astype(F32)).astype(BF16)
-    c_ref[0:TOK, :] = (dot(hi, rept) * keep).astype(BF16)
-    c_ref[TOK : 2 * TOK, :] = (dot(lo, rept) * keep).astype(BF16)
+    earlier = jnp.where(r < q, 1.0, 0.0).astype(BF16)
+    hits = hits.astype(BF16)
+    before = dot(hits, earlier).astype(BF16)
+    hi = weights.astype(BF16)
+    lo = (weights - hi.astype(F32)).astype(BF16)
+    for b in range(slots // 256):
+        s0 = lax.broadcasted_iota(jnp.int32, (256, 64), 0) + b * 256
+        e1 = lax.broadcasted_iota(jnp.int32, (256, 64), 1)
+        rep = jnp.where((s0 >> 4) == e1, 1.0, 0.0).astype(BF16)
+        lane = (lax.broadcasted_iota(jnp.int32, (256, TOK), 0) & 15).astype(F32)
+        keep = jnp.where(dot(rep, hits) > 0.5, jnp.where(dot(rep, before) == lane, 1.0, 0.0), 0.0)
+        at = slice(b * 256, (b + 1) * 256)
+        d_ref[at, :] = keep.astype(BF16)
+        c_ref[0:TOK, at] = jnp.transpose(dot(rep, hi) * keep).astype(BF16)
+        c_ref[TOK : 2 * TOK, at] = jnp.transpose(dot(rep, lo) * keep).astype(BF16)
 
 
 def layer_kernel(
+    q_hbm, k_hbm, v_hbm, qg_hbm, kg_hbm, cos_hbm, sin_hbm, wt_hbm,
+    hid_hbm, gain_hbm, idst_hbm, rwt_hbm, gate_ref, up_ref, down_ref,
+    out_ref,
     q_ref, k_ref, v_ref, qg_ref, kg_ref, cos_ref, sin_ref, wt_ref,
-    hid_ref, gain_ref, d_ref, c_ref, gate_ref, up_ref, down_ref,
-    out_ref,
+    hid_ref, gain_ref, idst_ref, rwt_ref, d_ref, c_ref, in_sem,
     qsend, kvsend, qbuf, qall, kvbuf, acc, den, ctx, wz, wfull, pstage, pbuf,
     resid, outb, inb, yb, retb, wg, wu, wd,
     q_s, q_r, kv_s, kv_r, up_s, up_r, dn_s, dn_r, sib_s, sib_r, wz_s, wz_r, wf_s, wf_r, p_s, p_r,
@@ -116,6 +103,14 @@
     inner = jnp.logical_not(source)
     p_ring = (z - g + ZN) % ZN
 
+    pairs = (
+        (q_hbm, q_ref), (k_hbm, k_ref), (v_hbm, v_ref), (qg_hbm, qg_ref), (kg_hbm, kg_ref), (cos_hbm, cos_ref),
+        (sin_hbm, sin_ref), (wt_hbm, wt_ref), (hid_hbm, hid_ref), (gain_hbm, gain_ref), (idst_hbm, idst_ref),
+        (rwt_hbm, rwt_ref),
+    )
+    loads = [pltpu.make_async_copy(src, dst, in_sem.at[i]) for i, (src, dst) in enumerate(pairs)]
+    for load in loads:
+        load.start()
     barrier = pltpu.get_barrier_semaphore()
 
     def loop(lo, hi, fn):
@@ -148,6 +143,8 @@
         for copy in own:
             copy.start()
 
+    for i in (1, 2, 4, 5, 6):
+        loads[i].wait()
     cosv = cos_ref[...]
     sinv = sin_ref[...]
 
@@ -160,30 +157,31 @@
     for h in range(2):
         kvsend[h, :, 0:128] = turned(k_ref[:, h * 128 : (h + 1) * 128], kg_ref[...])
         kvsend[h, :, 128:256] = v_ref[:, h * 128 : (h + 1) * 128]
+    pl.semaphore_wait(barrier, 46)
+
+    rows = pl.ds(pl.multiple_of((x % 2) * TOK, TOK), TOK)
+    dest_dp = y * 2 + x // 2
+
+    def to_chip(h, src, dst, send, recv):
+        here = jnp.logical_and(is_self, x % 2 == h)
+
+        @pl.when(here)
+        def _():
+            pltpu.make_async_copy(src, dst, recv).start()
+
+        @pl.when(jnp.logical_not(here))
+        def _():
+            copy_to(src, dst, send, recv, z * 4 + 2 * c + h, dest_dp).start()
+
+    for h in range(2):
+        to_chip(h, kvsend.at[h], kvbuf.at[z, x // 2, rows, :], kv_s.at[h], kv_r.at[x % 2])
+    for i in (0, 3, 7, 8, 9, 10, 11):
+        loads[i].wait()
     for h in range(2):
         for n in range(8):
             at = (h * 8 + n) * 128
             qsend[h, :, n * 128 : (n + 1) * 128] = turned(q_ref[:, at : at + 128], qg_ref[...])
-
-    pl.semaphore_wait(barrier, 46)
-
-    rows = pl.ds(pl.multiple_of((x % 2) * TOK, TOK), TOK)
-    dest_dp = y * 2 + x // 2
-    for h in range(2):
-        dest_sp = z * 4 + 2 * c + h
-        here = jnp.logical_and(is_self, x % 2 == h)
-        kv_dst = kvbuf.at[z, x // 2, rows, :]
-        q_dst = qbuf.at[x % 2]
-
-        @pl.when(here)
-        def _():
-            pltpu.make_async_copy(kvsend.at[h], kv_dst, kv_r.at[x % 2]).start()
-            pltpu.make_async_copy(qsend.at[h], q_dst, q_r.at[x % 2]).start()
-
-        @pl.when(jnp.logical_not(here))
-        def _():
-            copy_to(kvsend.at[h], kv_dst, kv_s.at[h], kv_r.at[x % 2], dest_sp, dest_dp).start()
-            copy_to(qsend.at[h], q_dst, q_s.at[h], q_r.at[x % 2], dest_sp, dest_dp).start()
+        to_chip(h, qsend.at[h], qbuf.at[x % 2], q_s.at[h], q_r.at[x % 2])
 
     def wz_copy(o):
         return copy_to(wt_ref, wz.at[own_k], wz_s.at[o], wz_r.at[own_k], ((z + o) % ZN) * 4 + x, g)
@@ -256,6 +254,8 @@
         loop(0, FIRST, one_dn)
 
 
+    route(idst_ref[...], rwt_ref[...], d_ref, c_ref)
+
     for t in range(2):
         kdst = kvbuf.at[z, c, pl.ds(t * TOK, TOK), :]
         pltpu.make_async_copy(kdst, kdst, kv_r.at[t]).wait()
@@ -272,8 +272,14 @@
         ref = kvbuf.at[slice_idx, half]
         return copy_to(ref, ref, sib_s.at[i], sib_r.at[i], sp, sib)
 
-    up_copy(1, z).start()
-    dn_copy(1, z).start()
+    @pl.when(z < ZN - 1)
+    def _():
+        up_copy(1, z).start()
+
+    @pl.when(z <= 6)
+    def _():
+        dn_copy(1, z).start()
+
     sib_copy(0, z, c).start()
 
     for t in range(2):
@@ -306,21 +312,49 @@
                 den[at, :] = den[at, :] + part
                 acc[at, :] = acc[at, :] + pv
 
+    for k in range(2):
+
+        @pl.when(jnp.logical_not(jnp.logical_and(source, own_k == k)))
+        def _():
+            pltpu.make_async_copy(wz.at[k], wz.at[k], wz_r.at[k]).wait()
+
+    def wf_copy(o):
+        t = (y * 4 + x + o) % 16
+        cols = pl.ds(pl.multiple_of((t % 2) * 1024, 1024), 1024)
+        return copy_to(
+            wz.at[:, :, cols], wfull.at[:, y, c, x], wf_s.at[o], wf_r.at[o], z * 4 + t % 4, (t // 4) * 2 + c
+        )
+
+    def wf_sib(half):
+        ref = wfull.at[:, :, half]
+        return copy_to(ref, ref, wf_s.at[0], wf_r.at[0], sp, sib)
+
+    loop(1, 16, lambda o: wf_copy(o).start())
+    mine = pl.ds(pl.multiple_of((x % 2) * 1024, 1024), 1024)
+    local = pltpu.make_async_copy(wz.at[:, :, mine], wfull.at[:, y, c, x], loc.at[0])
+    local.start()
+
     sib_copy(0, z, 1 - c).wait_recv()
     attend(z, True)
 
     def step(s):
         below = (z - s + ZN) % ZN
         above = (z + s) % ZN
-        up_copy(s, below).wait_recv()
-
-        @pl.when(s < 8)
-        def _():
-            up_copy(s + 1, below).start()
-
-        sib_copy(2 * s, below, c).start()
-
-        @pl.when(s < 8)
+        from_below = z >= s
+        above_on = jnp.logical_and(s < 8, jnp.logical_or(z + s <= 6, z + s >= ZN))
+        above_used = jnp.logical_and(s < 8, z + s >= ZN)
+
+        @pl.when(from_below)
+        def _():
+            up_copy(s, below).wait_recv()
+
+            @pl.when(jnp.logical_and(s < 8, z < ZN - 1))
+            def _():
+                up_copy(s + 1, below).start()
+
+            sib_copy(2 * s, below, c).start()
+
+        @pl.when(above_on)
         def _():
             dn_copy(s, above).wait_recv()
 
@@ -328,65 +362,40 @@
             def _():
                 dn_copy(s + 1, above).start()
 
+        @pl.when(above_used)
+        def _():
             sib_copy(2 * s + 1, above, c).start()
 
         ring(s - 1)
-        sib_copy(2 * s, below, 1 - c).wait_recv()
-
-        @pl.when(z >= s)
-        def _():
+
+        @pl.when(from_below)
+        def _():
+            sib_copy(2 * s, below, 1 - c).wait_recv()
             attend(below, False)
 
-        @pl.when(s < 8)
+        @pl.when(above_used)
         def _():
             sib_copy(2 * s + 1, above, 1 - c).wait_recv()
-
-            @pl.when(z + s >= ZN)
-            def _():
-                attend(above, False)
-
-    loop(1, 5, step)
-
-    for k in range(2):
-
-        @pl.when(jnp.logical_not(jnp.logical_and(source, own_k == k)))
-        def _():
-            pltpu.make_async_copy(wz.at[k], wz.at[k], wz_r.at[k]).wait()
-
-    def wf_copy(o):
-        t, psp, pdp = slice_peer(o)
-        cols = pl.ds(pl.multiple_of((t % 2) * 1024, 1024), 1024)
-        return copy_to(wz.at[:, :, cols], wfull.at[:, q_idx], wf_s.at[o], wf_r.at[o], psp, pdp)
-
-    loop(1, 32, lambda o: wf_copy(o).start())
-    mine = pl.ds(pl.multiple_of((x % 2) * 1024, 1024), 1024)
-    local = pltpu.make_async_copy(wz.at[:, :, mine], wfull.at[:, q_idx], loc.at[0])
-    local.start()
-
-    loop(5, 9, step)
+            attend(above, False)
+
+    loop(1, 6, step)
+    loop(1, 16, lambda o: wf_copy(o).wait_recv())
+    local.wait()
+    wf_sib(c).start()
+    loop(6, 9, step)
 
     for n in range(8):
         at = slice(n * 192, (n + 1) * 192)
         total = jnp.sum(den[at, :], axis=-1, keepdims=True)
         ctx[:, n * 128 : (n + 1) * 128] = (acc[at, :] / total).astype(BF16)
-    local.wait()
-    loop(1, 32, lambda o: wf_copy(o).wait_recv())
+    wf_sib(1 - c).wait_recv()
     for b in range(4):
-        w = wfull[b // 2, (b % 2) * 16 : (b % 2 + 1) * 16].reshape(256, 1024)
+        w = wfull[b // 2, (b % 2) * 2 : (b % 2 + 1) * 2].reshape(256, 1024)
         part = dot_nt(ctx[...], w).astype(BF16)
         for t in range(2):
             pstage[t, :, b * 256 : (b + 1) * 256] = part[t * TOK : (t + 1) * TOK, :]
     for t in range(2):
-        here = jnp.logical_and(is_self, x % 2 == t)
-        dst = pbuf.at[x % 2]
-
-        @pl.when(here)
-        def _():
-            pltpu.make_async_copy(pstage.at[t], dst, p_r.at[x % 2]).start()
-
-        @pl.when(jnp.logical_not(here))
-        def _():
-            copy_to(pstage.at[t], dst, p_s.at[t], p_r.at[x % 2], z * 4 + 2 * c + t, dest_dp).start()
+        to_chip(t, pstage.at[t], pbuf.at[x % 2], p_s.at[t], p_r.at[x % 2])
 
     ring(8)
     ring(9)
@@ -399,18 +408,37 @@
     ms = jnp.mean(res * res, axis=-1, keepdims=True)
     normed = (res * lax.rsqrt(ms + EPS) * gain_ref[...]).astype(BF16)
 
-    def there(o):
+    def first_of(dp):
+        return (((z - dp + ZN) % ZN + 3) // 8) % 2
+
+    def there(o, r):
         t, psp, pdp = slice_peer(o)
-        return copy_to(outb.at[t], inb.at[:, q_idx], a_s.at[o], a_r.at[o], psp, pdp)
-
-    def back(o):
+        kk = (first_of(pdp) + r) % 2
+        return copy_to(outb.at[t, kk], inb.at[kk, q_idx], a_s.at[r, o], a_r.at[r, o], psp, pdp)
+
+    def back(o, r):
         t, psp, pdp = slice_peer(o)
-        return copy_to(yb.at[:, t], retb.at[q_idx], b_s.at[o], b_r.at[o], psp, pdp)
+        kk = (first_of(g) + r) % 2
+        return copy_to(yb.at[kk, t], retb.at[q_idx, kk], b_s.at[r, o], b_r.at[r, o], psp, pdp)
+
+    def run_expert(r):
+        kk = (first_of(g) + r) % 2
+        loop(1, 32, lambda o: there(o, r).wait_recv())
+        tokens = inb[kk].reshape(512, 1024)
+        gate = dot(tokens, wg[kk])
+        upv = dot(tokens, wu[kk])
+        mid = (gate / (1.0 + jnp.exp(-gate)) * upv).astype(BF16)
+        yb[kk] = dot(mid, wd[kk]).astype(BF16).reshape(32, SLOT, 1024)
+        loop(1, 32, lambda o: back(o, r).start())
+        keep = pltpu.make_async_copy(yb.at[kk, q_idx], retb.at[q_idx, kk], loc.at[2 + r])
+        keep.start()
+        return keep
 
     for b in range(4):
         part = dot(d_ref[b * 256 : (b + 1) * 256, :], normed).astype(BF16)
         outb[b * 8 : (b + 1) * 8] = part.reshape(8, 2, SLOT, 1024)
-    loop(1, 32, lambda o: there(o).start())
+    loop(1, 32, lambda o: there(o, 0).start())
+    loop(1, 32, lambda o: there(o, 1).start())
     keep = pltpu.make_async_copy(outb.at[q_idx], inb.at[:, q_idx], loc.at[1])
     keep.start()
 
@@ -422,23 +450,16 @@
             def _():
                 act(j)
 
-    loop(FIRST + PER_STEP * 10, NPIECE + PER_HOP * 7, rest)
+    loop(FIRST + PER_STEP * 10, NPIECE + PER_HOP * 4, rest)
+    keep.wait()
+    keep_first = run_expert(0)
+    loop(NPIECE + PER_HOP * 4, NPIECE + PER_HOP * 7, rest)
 
     @pl.when(source)
     def _():
         loop(0, NPIECE, lambda j: piece(j, lambda ref: wup(ref(k_up_in), j).wait_recv()))
 
-    keep.wait()
-    loop(1, 32, lambda o: there(o).wait_recv())
-    for k in range(2):
-        tokens = inb[k].reshape(512, 1024)
-        gate = dot(tokens, wg[k])
-        upv = dot(tokens, wu[k])
-        mid = (gate / (1.0 + jnp.exp(-gate)) * upv).astype(BF16)
-        yb[k] = dot(mid, wd[k]).astype(BF16).reshape(32, SLOT, 1024)
-    loop(1, 32, lambda o: back(o).start())
-    keep2 = pltpu.make_async_copy(yb.at[:, q_idx], retb.at[q_idx], loc.at[2])
-    keep2.start()
+    keep_second = run_expert(1)
 
     @pl.when(source)
     def _():
@@ -450,11 +471,28 @@
     def _():
         loop(0, NPIECE, lambda j: piece(j, lambda ref: wdn(ref(k_dn), j).wait_send()))
 
-    loop(1, 32, lambda o: wf_copy(o).wait_send())
-    loop(1, 9, lambda s: up_copy(s, z).wait_send())
-    loop(1, 8, lambda s: dn_copy(s, z).wait_send())
+    loop(1, 16, lambda o: wf_copy(o).wait_send())
+    wf_sib(c).wait_send()
+
+    def kv_sent(s):
+        @pl.when(jnp.logical_and(z >= s - 1, z < ZN - 1))
+        def _():
+            up_copy(s, z).wait_send()
+
+        @pl.when(jnp.logical_and(s < 8, jnp.logical_or(z + s <= 7, z + s >= ZN + 1)))
+        def _():
+            dn_copy(s, z).wait_send()
+
+        @pl.when(z >= s)
+        def _():
+            sib_copy(2 * s, z, c).wait_send()
+
+        @pl.when(jnp.logical_and(s < 8, z + s >= ZN))
+        def _():
+            sib_copy(2 * s + 1, z, c).wait_send()
+
     sib_copy(0, z, c).wait_send()
-    loop(2, 17, lambda i: sib_copy(i, z, c).wait_send())
+    loop(1, 9, kv_sent)
     for h in range(2):
         here = jnp.logical_and(is_self, x % 2 == h)
 
@@ -466,12 +504,16 @@
             copy_to(qsend.at[h], qbuf.at[x % 2], q_s.at[h], q_r.at[x % 2], dest_sp, dest_dp).wait_send()
             copy_to(pstage.at[h], pbuf.at[x % 2], p_s.at[h], p_r.at[x % 2], dest_sp, dest_dp).wait_send()
 
-    loop(1, 32, lambda o: there(o).wait_send())
-    keep2.wait()
-    loop(1, 32, lambda o: back(o).wait_recv())
+    for r in range(2):
+        loop(1, 32, lambda o, r=r: there(o, r).wait_send())
+    keep_first.wait()
+    keep_second.wait()
+    for r in range(2):
+        loop(1, 32, lambda o, r=r: back(o, r).wait_recv())
     mixed = dot(c_ref[...], retb[...].reshape(1024, 1024))
     out_ref[...] = (resid[...] + (mixed[0:TOK, :] + mixed[TOK : 2 * TOK, :])).astype(BF16)
-    loop(1, 32, lambda o: back(o).wait_send())
+    for r in range(2):
+        loop(1, 32, lambda o, r=r: back(o, r).wait_send())
 
 
 def body(
@@ -488,23 +530,30 @@
     cos2 = jnp.concatenate([cosv, cosv], axis=-1)
     sin2 = jnp.concatenate([-sinv, sinv], axis=-1)
     vm = pl.BlockSpec(memory_space=pltpu.VMEM)
-    hbm = pl.BlockSpec(memory_space=pl.ANY)
+    hbm = pl.BlockSpec(memory_space=pltpu.HBM)
     dma = pltpu.SemaphoreType.DMA
-
-    disp, comb = pl.pallas_call(
-        route_kernel,
-        out_shape=(jax.ShapeDtypeStruct((1024, TOK), BF16), jax.ShapeDtypeStruct((2 * TOK, 1024), BF16)),
-        in_specs=[vm] * 3,
-        out_specs=(vm, vm),
-        name="route",
-    )(expert_ids, expert_ids.T, route_weights)
 
     return pl.pallas_call(
         layer_kernel,
         out_shape=jax.ShapeDtypeStruct((TOK, 1024), BF16),
-        in_specs=[vm] * 12 + [hbm] * 3,
+        in_specs=[hbm] * 15,
         out_specs=vm,
         scratch_shapes=[
+            pltpu.VMEM((TOK, 2048), BF16),
+            pltpu.VMEM((TOK, 256), BF16),
+            pltpu.VMEM((TOK, 256), BF16),
+            pltpu.VMEM((1, 128), F32),
+            pltpu.VMEM((1, 128), F32),
+            pltpu.VMEM((TOK, 128), F32),
+            pltpu.VMEM((TOK, 128), F32),
+            pltpu.VMEM((16, 2048), BF16),
+            pltpu.VMEM((TOK, 1024), BF16),
+            pltpu.VMEM((1, 1024), F32),
+            pltpu.VMEM((8, TOK), jnp.int32),
+            pltpu.VMEM((8, TOK), F32),
+            pltpu.VMEM((64 * SLOT, TOK), BF16),
+            pltpu.VMEM((2 * TOK, 64 * SLOT), BF16),
+            dma((12,)),
             pltpu.VMEM((2, TOK, 1024), BF16),
             pltpu.VMEM((2, TOK, 256), BF16),
             pltpu.VMEM((2, TOK, 1024), BF16),
@@ -514,7 +563,7 @@
             pltpu.VMEM((1536, 128), F32),
             pltpu.VMEM((192, 1024), BF16),
             pltpu.VMEM((2, 16, 2048), BF16),
-            pltpu.VMEM((2, 32, 16, 1024), BF16),
+            pltpu.VMEM((2, 4, 2, 4, 16, 1024), BF16),
             pltpu.VMEM((2, TOK, 1024), BF16),
             pltpu.VMEM((2, TOK, 1024), BF16),
             pltpu.VMEM((TOK, 1024), F32),
@@ -528,19 +577,19 @@
             dma((2,)), dma((2,)), dma((2,)), dma((2,)),
             dma((9,)), dma((9,)), dma((9,)), dma((9,)),
             dma((17,)), dma((17,)),
-            dma((16,)), dma((2,)), dma((32,)), dma((32,)),
-            dma((2,)), dma((2,)), dma((3,)),
+            dma((16,)), dma((2,)), dma((16,)), dma((16,)),
+            dma((2,)), dma((2,)), dma((4,)),
             dma((NPIECE,)), dma((NPIECE,)), dma((NPIECE,)), dma((NPIECE,)),
-            dma((3,)),
-            dma((32,)), dma((32,)), dma((32,)), dma((32,)),
+            dma((4,)),
+            dma((2, 32)), dma((2, 32)), dma((2, 32)), dma((2, 32)),
         ],
         compiler_params=pltpu.CompilerParams(
-            collective_id=0, has_side_effects=True, vmem_limit_bytes=48 * 1024 * 1024
+            collective_id=0, has_side_effects=True, vmem_limit_bytes=63 * 1024 * 1024
         ),
         name="layer",
     )(
         queries, keys, values, q_gain.reshape(1, 128), k_gain.reshape(1, 128), cos2, sin2, out_weight.T,
-        hidden_in, moe_gain.reshape(1, 1024), disp, comb, gate_proj[0], up_proj[0], down_proj[0],
+        hidden_in, moe_gain.reshape(1, 1024), expert_ids.T, route_weights.T, gate_proj[0], up_proj[0], down_proj[0],
     )
 
 

time: 195 us -> 153 us (0.78)
  the two profiles are of different devices: /device:TPU:21 before, /device:TPU:32 now
where the time goes in v2:
time: 153 us
  Pallas kernels  150 us (98%)
  local copies, waits for them, and re-layouts  1.62 us (1%)
    pallas_call x1, Pallas kernels, body(): pl.pallas_call(layer_kernel, out_shape=jax.ShapeDtypeStruct((TOK, 1024),...  150 us

profile of v2, /device:TPU:32, one launch (start us, length us, event | category | flops | bytes accessed | tf_op | source)
XLA Modules:
  0.0 152.8 jit_solution(15090274636950332602)
XLA Ops:
  0.0 0.3 fusion
  0.3 0.7 pad_maximum_fusion
  1.0 150.1 %layer.1 = bf16[96,1024]{1,0:T(8,128)(2,1)} custom-call(bf16[96,2048]{1,0:T(8,128)(2,1)} %q_hbm.1, bf16[96,256]{1,0:T(8,128)(2,1)} %k_hbm.1, bf16[96,256]{1,0:T(8,128)(2,1)} %v_hbm.1, f32[1,128]{1,0:T(1,128)} %bitcast.16, f32[1,128]{1,0:T(1,128)} %bitcast.17, f32[96,128]{1,0:T(8,128)} %get-tuple-element.8.cos_hbm, f32[96,128]{1,0:T(8,128)} %get-tuple-element.9.sin_hbm, ...), custom_call_target="tpu_custom_call" | custom-call | tf_op jit(solution)/shard_map/layer/pallas_call | solution.py:536
  151.1 1.6 %copy.15 = bf16[96,1024]{1,0:T(8,128)(2,1)} copy(bf16[96,1024]{1,0:T(8,128)(2,1)} %layer.1) | data formatting | bytes 393216
  (2 shorter events, 0.0 us)

commit v3 on v2

--- a/solution.py
+++ b/solution.py
@@ -19,7 +19,8 @@
 SLOT = 16
 PIECES = ((64, 16), (64, 16), (32, 12))
 NPIECE = 44
-FIRST, PER_STEP, PER_HOP = 6, 2, 3
+FIRST, PER_STEP, LAG = 6, 2, 6
+STEPS = 16
 NT = (((1,), (1,)), ((), ()))
 
 
@@ -159,6 +160,81 @@
         kvsend[h, :, 128:256] = v_ref[:, h * 128 : (h + 1) * 128]
     pl.semaphore_wait(barrier, 46)
 
+    k_up = p_ring // 8
+    k_dn = jnp.where(source, k_up, 1 - k_up)
+    k_up_in = ((p_ring + ZN - 1) % ZN) // 8
+    far_up = p_ring % 8
+    far_dn = (ZN - p_ring) % 8
+    down = far_dn != 7
+
+    hop = p_ring % 8
+
+    def wz_copy(n, k, shift):
+        ref = wz.at[k]
+        return copy_to(ref, ref, wz_s.at[n], wz_r.at[k], ((z + shift + ZN) % ZN) * 4 + x, g)
+
+    routes = ((0, k_up, (2, 5, -2, -5)), (2, k_up, (-1, 1)), (5, k_up, (-1, 1, 2, 3)), (6, k_dn, (1, -1)), (3, k_dn, (1, -1, -2)))
+
+    def wz_wait(k):
+        pltpu.make_async_copy(wz.at[k], wz.at[k], wz_r.at[k]).wait()
+
+    def wz_run(which, fn):
+        for at, k, shifts in which:
+
+            @pl.when(hop == at)
+            def _():
+                for n, shift in enumerate(shifts):
+                    fn(wz_copy(n, k, shift))
+
+    def piece(j, fn):
+        at = 0
+        for store, (n_rows, count) in zip(stores, PIECES):
+            first = at
+
+            @pl.when(jnp.logical_and(j >= first, j < first + count))
+            def _():
+                start = pl.multiple_of((j - first) * n_rows, n_rows)
+                fn(lambda k: store.at[k, pl.ds(start, n_rows), :])
+
+            at += count
+
+    def wup(ref, j):
+        return copy_to(ref, ref, wup_s.at[j], wup_r.at[j], up_sp, g)
+
+    def wdn(ref, j):
+        return copy_to(ref, ref, wdn_s.at[j], wdn_r.at[j], dn_sp, g)
+
+    def one_up(j):
+        def act(ref):
+            @pl.when(inner)
+            def _():
+                wup(ref(k_up_in), j).wait_recv()
+
+            wup(ref(k_up), j).start()
+
+        piece(j, act)
+
+    def one_dn(j):
+        def act(ref):
+            @pl.when(inner)
+            def _():
+                wdn(ref(k_dn), j).wait_recv()
+
+            @pl.when(down)
+            def _():
+                wdn(ref(k_dn), j).start()
+
+        piece(j, act)
+
+    def reach(t, far):
+        return jnp.clip(FIRST + PER_STEP * t - LAG * far // 2, 0, NPIECE)
+
+    def ring(t):
+        for far, act in ((far_up, one_up), (far_dn, one_dn)):
+            lo = jnp.where(jnp.logical_and(t == 0, inner), 0, reach(t, far))
+            loop(lo, reach(t + 1, far), act)
+
+
     rows = pl.ds(pl.multiple_of((x % 2) * TOK, TOK), TOK)
     dest_dp = y * 2 + x // 2
 
@@ -175,7 +251,21 @@
 
     for h in range(2):
         to_chip(h, kvsend.at[h], kvbuf.at[z, x // 2, rows, :], kv_s.at[h], kv_r.at[x % 2])
-    for i in (0, 3, 7, 8, 9, 10, 11):
+    loads[7].wait()
+
+    @pl.when(source)
+    def _():
+        wz[own_k] = wt_ref[...]
+
+    wz_run(routes[:1], lambda copy: copy.start())
+    @pl.when(source)
+    def _():
+        for copy in own:
+            copy.wait()
+        loop(0, FIRST, one_up)
+        loop(0, FIRST, one_dn)
+
+    for i in (0, 3, 8, 9, 10, 11):
         loads[i].wait()
     for h in range(2):
         for n in range(8):
@@ -183,78 +273,16 @@
             qsend[h, :, n * 128 : (n + 1) * 128] = turned(q_ref[:, at : at + 128], qg_ref[...])
         to_chip(h, qsend.at[h], qbuf.at[x % 2], q_s.at[h], q_r.at[x % 2])
 
-    def wz_copy(o):
-        return copy_to(wt_ref, wz.at[own_k], wz_s.at[o], wz_r.at[own_k], ((z + o) % ZN) * 4 + x, g)
-
-    @pl.when(source)
-    def _():
-        wz[own_k] = wt_ref[...]
-        loop(1, ZN, lambda o: wz_copy(o).start())
-
-    k_up = p_ring // 8
-    k_dn = jnp.where(source, k_up, 1 - k_up)
-    k_up_in = ((p_ring + ZN - 1) % ZN) // 8
-    far_up = p_ring % 8
-    far_dn = (ZN - p_ring) % 8
-    down = far_dn != 7
-
-    def piece(j, fn):
-        at = 0
-        for store, (n_rows, count) in zip(stores, PIECES):
-            first = at
-
-            @pl.when(jnp.logical_and(j >= first, j < first + count))
-            def _():
-                start = pl.multiple_of((j - first) * n_rows, n_rows)
-                fn(lambda k: store.at[k, pl.ds(start, n_rows), :])
-
-            at += count
-
-    def wup(ref, j):
-        return copy_to(ref, ref, wup_s.at[j], wup_r.at[j], up_sp, g)
-
-    def wdn(ref, j):
-        return copy_to(ref, ref, wdn_s.at[j], wdn_r.at[j], dn_sp, g)
-
-    def one_up(j):
-        def act(ref):
-            @pl.when(inner)
-            def _():
-                wup(ref(k_up_in), j).wait_recv()
-
-            wup(ref(k_up), j).start()
-
-        piece(j, act)
-
-    def one_dn(j):
-        def act(ref):
-            @pl.when(inner)
-            def _():
-                wdn(ref(k_dn), j).wait_recv()
-
-            @pl.when(down)
-            def _():
-                wdn(ref(k_dn), j).start()
-
-        piece(j, act)
-
-    def reach(t, far):
-        return jnp.clip(FIRST + PER_STEP * t - PER_HOP * far, 0, NPIECE)
-
-    def ring(t):
-        for far, act in ((far_up, one_up), (far_dn, one_dn)):
-            lo = jnp.where(jnp.logical_and(t == 0, inner), 0, reach(t, far))
-            loop(lo, reach(t + 1, far), act)
-
-    @pl.when(source)
-    def _():
-        for copy in own:
-            copy.wait()
-        loop(0, FIRST, one_up)
-        loop(0, FIRST, one_dn)
-
-
     route(idst_ref[...], rwt_ref[...], d_ref, c_ref)
+    for n in range(1, 5):
+        at, k, _ = routes[n]
+
+        @pl.when(hop == at)
+        def _():
+            wz_wait(k)
+
+    wz_run(routes[1:], lambda copy: copy.start())
+    ring(0)
 
     for t in range(2):
         kdst = kvbuf.at[z, c, pl.ds(t * TOK, TOK), :]
@@ -288,6 +316,7 @@
         for t in range(2):
             qall[n * 192 + t * TOK : n * 192 + (t + 1) * TOK, :] = qbuf[t, :, n * 128 : (n + 1) * 128]
 
+    ring(1)
     factor = math.log2(math.e) / math.sqrt(128)
 
     def attend(slice_idx, diagonal):
@@ -312,11 +341,24 @@
                 den[at, :] = den[at, :] + part
                 acc[at, :] = acc[at, :] + pv
 
-    for k in range(2):
-
-        @pl.when(jnp.logical_not(jnp.logical_and(source, own_k == k)))
-        def _():
-            pltpu.make_async_copy(wz.at[k], wz.at[k], wz_r.at[k]).wait()
+    relay_up = jnp.logical_or(hop == 2, hop == 5)
+    relay_dn = jnp.logical_or(hop == 3, hop == 6)
+    @pl.when(relay_up)
+    def _():
+        wz_wait(k_dn)
+
+    @pl.when(relay_dn)
+    def _():
+        wz_wait(k_up)
+
+    @pl.when(source)
+    def _():
+        wz_wait(1 - own_k)
+
+    @pl.when(jnp.logical_not(jnp.logical_or(source, jnp.logical_or(relay_up, relay_dn))))
+    def _():
+        wz_wait(0)
+        wz_wait(1)
 
     def wf_copy(o):
         t = (y * 4 + x + o) % 16
@@ -336,6 +378,7 @@
 
     sib_copy(0, z, 1 - c).wait_recv()
     attend(z, True)
+    ring(2)
 
     def step(s):
         below = (z - s + ZN) % ZN
@@ -366,7 +409,7 @@
         def _():
             sib_copy(2 * s + 1, above, c).start()
 
-        ring(s - 1)
+        ring(s + 2)
 
         @pl.when(from_below)
         def _():
@@ -388,6 +431,7 @@
         at = slice(n * 192, (n + 1) * 192)
         total = jnp.sum(den[at, :], axis=-1, keepdims=True)
         ctx[:, n * 128 : (n + 1) * 128] = (acc[at, :] / total).astype(BF16)
+    ring(11)
     wf_sib(1 - c).wait_recv()
     for b in range(4):
         w = wfull[b // 2, (b % 2) * 2 : (b % 2 + 1) * 2].reshape(256, 1024)
@@ -397,8 +441,7 @@
     for t in range(2):
         to_chip(t, pstage.at[t], pbuf.at[x % 2], p_s.at[t], p_r.at[x % 2])
 
-    ring(8)
-    ring(9)
+    loop(12, STEPS, ring)
     for h in range(2):
         pltpu.make_async_copy(pbuf.at[h], pbuf.at[h], p_r.at[h]).wait()
 
@@ -444,16 +487,16 @@
 
     def rest(i):
         for far, act in ((far_up, one_up), (far_dn, one_dn)):
-            j = i - PER_HOP * far
+            j = i - LAG * far // 2
 
             @pl.when(jnp.logical_and(j >= 0, j < NPIECE))
             def _():
                 act(j)
 
-    loop(FIRST + PER_STEP * 10, NPIECE + PER_HOP * 4, rest)
+    loop(FIRST + PER_STEP * STEPS, NPIECE + LAG * 2, rest)
     keep.wait()
     keep_first = run_expert(0)
-    loop(NPIECE + PER_HOP * 4, NPIECE + PER_HOP * 7, rest)
+    loop(NPIECE + LAG * 2, NPIECE + LAG * 7 // 2, rest)
 
     @pl.when(source)
     def _():
@@ -461,10 +504,7 @@
 
     keep_second = run_expert(1)
 
-    @pl.when(source)
-    def _():
-        loop(1, ZN, lambda o: wz_copy(o).wait_send())
-
+    wz_run(routes, lambda copy: copy.wait_send())
     loop(0, NPIECE, lambda j: piece(j, lambda ref: wup(ref(k_up), j).wait_send()))
 
     @pl.when(down)
@@ -577,7 +617,7 @@
             dma((2,)), dma((2,)), dma((2,)), dma((2,)),
             dma((9,)), dma((9,)), dma((9,)), dma((9,)),
             dma((17,)), dma((17,)),
-            dma((16,)), dma((2,)), dma((16,)), dma((16,)),
+            dma((4,)), dma((2,)), dma((16,)), dma((16,)),
             dma((2,)), dma((2,)), dma((4,)),
             dma((NPIECE,)), dma((NPIECE,)), dma((NPIECE,)), dma((NPIECE,)),
             dma((4,)),

time: 153 us -> 141 us (0.922)
  the two profiles are of different devices: /device:TPU:32 before, /device:TPU:5 now
where the time goes in v3:
time: 141 us
  Pallas kernels  138 us (98%)
  local copies, waits for them, and re-layouts  1.62 us (1%)
    pallas_call x1, Pallas kernels, body(): pl.pallas_call(layer_kernel, out_shape=jax.ShapeDtypeStruct((TOK, 1024),...  138 us

profile of v3, /device:TPU:5, one launch (start us, length us, event | category | flops | bytes accessed | tf_op | source)
XLA Modules:
  0.0 140.6 jit_solution(2968170186667061608)
XLA Ops:
  0.0 0.3 fusion
  0.3 0.7 pad_maximum_fusion
  1.0 138.0 %layer.1 = bf16[96,1024]{1,0:T(8,128)(2,1)} custom-call(bf16[96,2048]{1,0:T(8,128)(2,1)} %q_hbm.1, bf16[96,256]{1,0:T(8,128)(2,1)} %k_hbm.1, bf16[96,256]{1,0:T(8,128)(2,1)} %v_hbm.1, f32[1,128]{1,0:T(1,128)} %bitcast.16, f32[1,128]{1,0:T(1,128)} %bitcast.17, f32[96,128]{1,0:T(8,128)} %get-tuple-element.8.cos_hbm, f32[96,128]{1,0:T(8,128)} %get-tuple-element.9.sin_hbm, ...), custom_call_target="tpu_custom_call" | custom-call | tf_op jit(solution)/shard_map/layer/pallas_call | solution.py:576
  139.0 1.6 %copy.15 = bf16[96,1024]{1,0:T(8,128)(2,1)} copy(bf16[96,1024]{1,0:T(8,128)(2,1)} %layer.1) | data formatting | bytes 393216
  (2 shorter events, 0.0 us)

commit v4 on v3

--- a/solution.py
+++ b/solution.py
@@ -17,9 +17,9 @@
 TOK = 96
 ZN = 16
 SLOT = 16
-PIECES = ((64, 16), (64, 16), (32, 12))
-NPIECE = 44
-FIRST, PER_STEP, LAG = 6, 2, 6
+PIECES = ((128, 8), (128, 8), (64, 6))
+NPIECE = 22
+FIRST, PER_STEP, LAG = 4, 1, 4
 STEPS = 16
 NT = (((1,), (1,)), ((), ()))
 
@@ -478,9 +478,18 @@
         return keep
 
     for b in range(4):
-        part = dot(d_ref[b * 256 : (b + 1) * 256, :], normed).astype(BF16)
-        outb[b * 8 : (b + 1) * 8] = part.reshape(8, 2, SLOT, 1024)
-    loop(1, 32, lambda o: there(o, 0).start())
+        quarter = (q_idx // 8 + b) % 4
+        part = dot(d_ref[pl.ds(pl.multiple_of(quarter * 256, 256), 256), :], normed).astype(BF16)
+        outb[pl.ds(quarter * 8, 8)] = part.reshape(8, 2, SLOT, 1024)
+
+        def leave(i, quarter=quarter):
+            o = (quarter * 8 + (q_idx + i) % 8 - q_idx + 32) % 32
+
+            @pl.when(o != 0)
+            def _():
+                there(o, 0).start()
+
+        loop(0, 8, leave)
     loop(1, 32, lambda o: there(o, 1).start())
     keep = pltpu.make_async_copy(outb.at[q_idx], inb.at[:, q_idx], loc.at[1])
     keep.start()

time: 141 us -> 141 us (level)
  the two profiles are of different devices: /device:TPU:5 before, /device:TPU:32 now
where the time goes in v4:
time: 141 us; the launch traced here: 140 us
  Pallas kernels  137 us (97%)
  local copies, waits for them, and re-layouts  1.62 us (1%)
    pallas_call x1, Pallas kernels, body(): pl.pallas_call(layer_kernel, out_shape=jax.ShapeDtypeStruct((TOK, 1024),...  137 us

profile of v4, /device:TPU:32, one launch (start us, length us, event | category | flops | bytes accessed | tf_op | source)
XLA Modules:
  0.0 140.0 jit_solution(10091166608922091303)
XLA Ops:
  0.0 0.3 fusion
  0.3 0.7 pad_maximum_fusion
  1.0 137.4 %layer.1 = bf16[96,1024]{1,0:T(8,128)(2,1)} custom-call(bf16[96,2048]{1,0:T(8,128)(2,1)} %q_hbm.1, bf16[96,256]{1,0:T(8,128)(2,1)} %k_hbm.1, bf16[96,256]{1,0:T(8,128)(2,1)} %v_hbm.1, f32[1,128]{1,0:T(1,128)} %bitcast.16, f32[1,128]{1,0:T(1,128)} %bitcast.17, f32[96,128]{1,0:T(8,128)} %get-tuple-element.8.cos_hbm, f32[96,128]{1,0:T(8,128)} %get-tuple-element.9.sin_hbm, ...), custom_call_target="tpu_custom_call" | custom-call | tf_op jit(solution)/shard_map/layer/pallas_call | solution.py:585
  138.4 1.6 %copy.15 = bf16[96,1024]{1,0:T(8,128)(2,1)} copy(bf16[96,1024]{1,0:T(8,128)(2,1)} %layer.1) | data formatting | bytes 393216
  (2 shorter events, 0.0 us)
